TPU v7x, 32 devices: a whole 2x2x4 slice. The times are simulated.
32 devices in a mesh: ax: 8 (over z, core), xs: 4 (over y, x).
Axes of the slice: x: 2, y: 2, z: 4, core: 2. Of those that a mesh axis runs over, the one named last changes fastest.
Arguments:
- scalar: float32 [64, 256, 1024], P('ax', 'xs'), may hold values from 0 to 1
- axial_rate: float32 [64, 256, 1024], P('ax', 'xs'), may hold values from 1.1 to 2.4
- swirl_rate: float32 [64, 256, 1024], P('ax', 'xs'), may hold values from -4 to 4
Outputs:
- transported: float32 [64, 256, 1024], P('ax', 'xs')
All inputs are finite; a program needn't handle non-finite values.
Results may differ from a plain program's by a relative error of at most 0.00014.
Values sent between devices are 32-bit elements; how exact they have to be, the bound alone decides.
A program may use at most 64 MiB of HBM per device.

v0:
```python
import math

import jax
import jax.numpy as jnp
from jax import lax
from jax.sharding import PartitionSpec as P

CZ = 8
SUBSTEPS = 2


axial_weight = 0.2
azimuth_damp = 0.5
diffusion_number = 1.0
stencil_coeffs = (
    -1.0 / 560.0,
    8.0 / 315.0,
    -0.2,
    1.6,
    -205.0 / 72.0,
    1.6,
    -0.2,
    8.0 / 315.0,
    -1.0 / 560.0,
)


def with_halo(block, sides, width):
    for axis, dim in sides:
        count = lax.axis_size(axis)
        forward = [(i, i + 1) for i in range(count - 1)]
        backward = [(target, source) for source, target in forward]
        low = lax.ppermute(
            lax.slice_in_dim(block, block.shape[dim] - width, None, axis=dim), axis, forward
        )
        high = lax.ppermute(lax.slice_in_dim(block, 0, width, axis=dim), axis, backward)
        block = jnp.concatenate([low, block, high], axis=dim)
    return block


def from_behind(value, axis, steps):
    count = lax.axis_size(axis)
    initial, last = (max(0, -steps), min(count, count - steps))
    return lax.ppermute(value, axis, [(source, source + steps) for source in range(initial, last)])


def radial_bands(cell_count, diffusion_value):
    cell_index = jnp.arange(cell_count, dtype=jnp.float32)
    radius = cell_index + 0.5
    upper_face = jnp.where(cell_index < cell_count - 1, cell_index + 1.0, 0.0)
    sub_diag = -diffusion_value * cell_index / radius
    super_diag = -diffusion_value * upper_face / radius
    main_diag = 1.0 - sub_diag - super_diag
    return (sub_diag, main_diag, super_diag)


def azimuth_tables(point_count):
    nyquist = point_count // 2
    column = jnp.arange(point_count, dtype=jnp.int32)
    cosine_cols = column <= nyquist
    wavenum = jnp.where(cosine_cols, column, column - nyquist)
    grid_point = jnp.arange(point_count, dtype=jnp.int32)
    phase_index = grid_point[:, None] * wavenum[None, :] % point_count
    angle_rad = phase_index.astype(jnp.float32) * (2.0 * math.pi / point_count)
    cosine = jnp.cos(angle_rad)
    sine_table = jnp.sin(angle_rad)
    forward = jnp.where(cosine_cols[None, :], cosine, sine_table)
    weight = jnp.where((wavenum == 0) | (wavenum == nyquist), 1.0, 2.0) / point_count
    inverse_smooth = jnp.transpose(forward * weight[None, :])
    slope_rate = wavenum.astype(jnp.float32) * (2.0 * math.pi / point_count) * (2.0 / point_count)
    slope_rate = jnp.where(cosine_cols & (wavenum == nyquist), 0.0, slope_rate)
    derivative = jnp.where(
        cosine_cols[None, :], -slope_rate[None, :] * sine_table, slope_rate[None, :] * cosine
    )
    inverse = jnp.concatenate([inverse_smooth, jnp.transpose(derivative)], axis=1)
    return (forward, inverse, wavenum)


def combine_pairs(earlier, later):
    return (earlier[0] * later[0], later[0] * earlier[1] + later[1])


def apply_lines(matrix, lines):
    return jnp.einsum(
        "ri,zic->zrc",
        matrix,
        lines,
        precision=lax.Precision.HIGHEST,
        preferred_element_type=jnp.float32,
    )


def body(scalar, axial_rate, swirl_rate):
    plane_count, radial_rows, azimuth_points = scalar.shape
    group_count = lax.axis_size("xs")
    radii_all = radial_rows * group_count
    forward, inverse, wavenum = azimuth_tables(azimuth_points)
    group_index = lax.axis_index("xs")
    first_row = group_index * radial_rows
    radius = (first_row + jnp.arange(radial_rows, dtype=jnp.int32)).astype(jnp.float32) + 0.5
    damping = 1.0 / (
        1.0
        + azimuth_damp
        * jnp.square(wavenum.astype(jnp.float32))[None, :]
        / jnp.square(radius)[:, None]
    )
    courant = CZ * axial_rate
    factor = courant / (1.0 + courant)
    sub_diag, main_diag, super_diag = radial_bands(radii_all, diffusion_number)
    green = lax.linalg.tridiagonal_solve(
        sub_diag, main_diag, super_diag, jnp.eye(radii_all, dtype=jnp.float32)
    )
    field_now = scalar
    for substep in range(SUBSTEPS):
        padded = with_halo(field_now, (("ax", 0),), 4)
        stencil_sum = jnp.zeros_like(field_now)
        for offset in range(9):
            stencil_sum = (
                stencil_sum + stencil_coeffs[offset] * padded[offset : offset + plane_count]
            )
        explicit_field = field_now + axial_weight * stencil_sum
        result = apply_lines(
            green, lax.all_to_all(explicit_field, "xs", split_axis=2, concat_axis=1, tiled=True)
        )
        solved = lax.all_to_all(result, "xs", split_axis=1, concat_axis=2, tiled=True)
        spectrum = jnp.dot(
            solved, forward, precision=lax.Precision.HIGHEST, preferred_element_type=jnp.float32
        )
        spectrum = spectrum * damping
        physical = jnp.dot(
            spectrum, inverse, precision=lax.Precision.HIGHEST, preferred_element_type=jnp.float32
        )
        smooth = physical[..., :azimuth_points]
        azimuth_slope = physical[..., azimuth_points:]
        source = smooth - swirl_rate * azimuth_slope
        scaled = source / (1.0 + courant)
        decay_prod, partial_value = lax.associative_scan(combine_pairs, (factor, scaled), axis=0)
        total_decay = decay_prod[-1]
        total_value = partial_value[-1]

        def relay_turn(turn_index, entering):
            return from_behind(total_decay * entering + total_value, "ax", 1)

        incoming = lax.fori_loop(
            0, lax.axis_size("ax") - 1, relay_turn, jnp.zeros_like(total_value)
        )
        field_now = partial_value + decay_prod * incoming
    return field_now


def solution(mesh):
    return jax.shard_map(
        body,
        mesh=mesh,
        in_specs=(P("ax", "xs", None), P("ax", "xs", None), P("ax", "xs", None)),
        out_specs=P("ax", "xs", None),
        check_vma=False,
    )
```

profile of v0, /device:TPU:1, one launch (start us, length us, event | category | flops | bytes accessed | tf_op | source)
XLA Modules:
  0.0 1319.1 jit_solution(14513097711449947912)
XLA Ops:
  16.5 596.7 %while.52 = (s32[]{:T(128)}, f32[]{:T(128)}, f32[256]{0:T(256)S(1)}, f32[7,32]{1,0:T(8,128)S(1)}, f32[7,32,256]{2,1,0:T(8,128)S(1)}, /*index=5*/f32[7,32]{1,0:T(...) while((s32[]{:T(128)}, f32[]{:T(128)}, ...), condition=%wide.region_1.2_spmd, body=%wide.region_0.1_spmd.sunk | while | flops 24705 | bytes 269565 | solution.py:110
  81.1 20.3 %subtract_divide_fusion.125 = (f32[256]{0:T(256)S(1)}, f32[256]{0:T(256)S(1)}, f32[256]{0:T(256)S(1)}, f32[256]{0:T(256)S(1)}, f32[256]{0:T(256)S(1)}, /*index=5...) fusion(f32[256]{0:T(256)S(1)} %bitcast.1275, ...), kind=kLoop, calls=%fused_computation.36.clone.1 | loop fusion | flops 24576 | bytes 66816 | tf_op jit(solution)/shard_map/while/body/eval_jaxpr/div | solution.py:110
  166.3 20.3 %subtract_divide_fusion.125 = (f32[256]{0:T(256)S(1)}, f32[256]{0:T(256)S(1)}, f32[256]{0:T(256)S(1)}, f32[256]{0:T(256)S(1)}, f32[256]{0:T(256)S(1)}, /*index=5...) fusion(f32[256]{0:T(256)S(1)} %bitcast.1275, ...), kind=kLoop, calls=%fused_computation.36.clone.1 | loop fusion | flops 24576 | bytes 66816 | tf_op jit(solution)/shard_map/while/body/eval_jaxpr/div | solution.py:110
  251.6 20.3 %subtract_divide_fusion.125 = (f32[256]{0:T(256)S(1)}, f32[256]{0:T(256)S(1)}, f32[256]{0:T(256)S(1)}, f32[256]{0:T(256)S(1)}, f32[256]{0:T(256)S(1)}, /*index=5...) fusion(f32[256]{0:T(256)S(1)} %bitcast.1275, ...), kind=kLoop, calls=%fused_computation.36.clone.1 | loop fusion | flops 24576 | bytes 66816 | tf_op jit(solution)/shard_map/while/body/eval_jaxpr/div | solution.py:110
  336.8 20.3 %subtract_divide_fusion.125 = (f32[256]{0:T(256)S(1)}, f32[256]{0:T(256)S(1)}, f32[256]{0:T(256)S(1)}, f32[256]{0:T(256)S(1)}, f32[256]{0:T(256)S(1)}, /*index=5...) fusion(f32[256]{0:T(256)S(1)} %bitcast.1275, ...), kind=kLoop, calls=%fused_computation.36.clone.1 | loop fusion | flops 24576 | bytes 66816 | tf_op jit(solution)/shard_map/while/body/eval_jaxpr/div | solution.py:110
  422.1 20.3 %subtract_divide_fusion.125 = (f32[256]{0:T(256)S(1)}, f32[256]{0:T(256)S(1)}, f32[256]{0:T(256)S(1)}, f32[256]{0:T(256)S(1)}, f32[256]{0:T(256)S(1)}, /*index=5...) fusion(f32[256]{0:T(256)S(1)} %bitcast.1275, ...), kind=kLoop, calls=%fused_computation.36.clone.1 | loop fusion | flops 24576 | bytes 66816 | tf_op jit(solution)/shard_map/while/body/eval_jaxpr/div | solution.py:110
  507.3 20.3 %subtract_divide_fusion.125 = (f32[256]{0:T(256)S(1)}, f32[256]{0:T(256)S(1)}, f32[256]{0:T(256)S(1)}, f32[256]{0:T(256)S(1)}, f32[256]{0:T(256)S(1)}, /*index=5...) fusion(f32[256]{0:T(256)S(1)} %bitcast.1275, ...), kind=kLoop, calls=%fused_computation.36.clone.1 | loop fusion | flops 24576 | bytes 66816 | tf_op jit(solution)/shard_map/while/body/eval_jaxpr/div | solution.py:110
  592.6 20.3 %subtract_divide_fusion.125 = (f32[256]{0:T(256)S(1)}, f32[256]{0:T(256)S(1)}, f32[256]{0:T(256)S(1)}, f32[256]{0:T(256)S(1)}, f32[256]{0:T(256)S(1)}, /*index=5...) fusion(f32[256]{0:T(256)S(1)} %bitcast.1275, ...), kind=kLoop, calls=%fused_computation.36.clone.1 | loop fusion | flops 24576 | bytes 66816 | tf_op jit(solution)/shard_map/while/body/eval_jaxpr/div | solution.py:110
  670.7 19.2 %subtract_divide_fusion.32 = (f32[256]{0:T(256)S(1)}, f32[256]{0:T(256)S(1)}, f32[256]{0:T(256)S(1)}, f32[256]{0:T(256)S(1)}, f32[256]{0:T(256)S(1)}, /*index=5*...) fusion(f32[256]{0:T(256)S(1)} %bitcast.1480, ...), kind=kLoop, calls=%fused_computation.337 | loop fusion | flops 23808 | bytes 64760 | tf_op jit(solution)/shard_map/eval_jaxpr/div | solution.py:110
  691.0 154.7 %while.53 = (s32[]{:T(128)}, f32[256]{0:T(256)S(1)}, f32[7,32,256]{2,1,0:T(8,128)}, f32[7,32,256]{2,1,0:T(8,128)S(1)}, f32[7,32]{1,0:T(8,128)S(1)}, /*index=5*/s...) while((s32[]{:T(128)}, f32[256]{0:T(256)S(1)}, ...), condition=%wide.region_3.4_spmd, body=%wide.region_2.3_spmd.sunk | while | flops 16418 | bytes 266721 | solution.py:110
  692.6 19.8 %multiply_subtract_fusion.125 = (f32[256]{0:T(256)S(1)}, f32[256]{0:T(256)S(1)}, f32[256]{0:T(256)S(1)}, f32[256]{0:T(256)S(1)}, f32[256]{0:T(256)S(1)}, /*index...) fusion(f32[256]{0:T(256)S(1)} %bitcast.1342, ...), kind=kLoop, calls=%fused_computation.102.clone.1 | loop fusion | flops 16384 | bytes 66688 | tf_op jit(solution)/shard_map/while/body/eval_jaxpr/sub | solution.py:110
  714.7 19.8 %multiply_subtract_fusion.125 = (f32[256]{0:T(256)S(1)}, f32[256]{0:T(256)S(1)}, f32[256]{0:T(256)S(1)}, f32[256]{0:T(256)S(1)}, f32[256]{0:T(256)S(1)}, /*index...) fusion(f32[256]{0:T(256)S(1)} %bitcast.1342, ...), kind=kLoop, calls=%fused_computation.102.clone.1 | loop fusion | flops 16384 | bytes 66688 | tf_op jit(solution)/shard_map/while/body/eval_jaxpr/sub | solution.py:110
  736.8 19.8 %multiply_subtract_fusion.125 = (f32[256]{0:T(256)S(1)}, f32[256]{0:T(256)S(1)}, f32[256]{0:T(256)S(1)}, f32[256]{0:T(256)S(1)}, f32[256]{0:T(256)S(1)}, /*index...) fusion(f32[256]{0:T(256)S(1)} %bitcast.1342, ...), kind=kLoop, calls=%fused_computation.102.clone.1 | loop fusion | flops 16384 | bytes 66688 | tf_op jit(solution)/shard_map/while/body/eval_jaxpr/sub | solution.py:110
  758.9 19.8 %multiply_subtract_fusion.125 = (f32[256]{0:T(256)S(1)}, f32[256]{0:T(256)S(1)}, f32[256]{0:T(256)S(1)}, f32[256]{0:T(256)S(1)}, f32[256]{0:T(256)S(1)}, /*index...) fusion(f32[256]{0:T(256)S(1)} %bitcast.1342, ...), kind=kLoop, calls=%fused_computation.102.clone.1 | loop fusion | flops 16384 | bytes 66688 | tf_op jit(solution)/shard_map/while/body/eval_jaxpr/sub | solution.py:110
  781.0 19.8 %multiply_subtract_fusion.125 = (f32[256]{0:T(256)S(1)}, f32[256]{0:T(256)S(1)}, f32[256]{0:T(256)S(1)}, f32[256]{0:T(256)S(1)}, f32[256]{0:T(256)S(1)}, /*index...) fusion(f32[256]{0:T(256)S(1)} %bitcast.1342, ...), kind=kLoop, calls=%fused_computation.102.clone.1 | loop fusion | flops 16384 | bytes 66688 | tf_op jit(solution)/shard_map/while/body/eval_jaxpr/sub | solution.py:110
  803.1 19.8 %multiply_subtract_fusion.125 = (f32[256]{0:T(256)S(1)}, f32[256]{0:T(256)S(1)}, f32[256]{0:T(256)S(1)}, f32[256]{0:T(256)S(1)}, f32[256]{0:T(256)S(1)}, /*index...) fusion(f32[256]{0:T(256)S(1)} %bitcast.1342, ...), kind=kLoop, calls=%fused_computation.102.clone.1 | loop fusion | flops 16384 | bytes 66688 | tf_op jit(solution)/shard_map/while/body/eval_jaxpr/sub | solution.py:110
  825.2 19.8 %multiply_subtract_fusion.125 = (f32[256]{0:T(256)S(1)}, f32[256]{0:T(256)S(1)}, f32[256]{0:T(256)S(1)}, f32[256]{0:T(256)S(1)}, f32[256]{0:T(256)S(1)}, /*index...) fusion(f32[256]{0:T(256)S(1)} %bitcast.1342, ...), kind=kLoop, calls=%fused_computation.102.clone.1 | loop fusion | flops 16384 | bytes 66688 | tf_op jit(solution)/shard_map/while/body/eval_jaxpr/sub | solution.py:110
  866.5 19.4 %multiply_subtract_fusion.32 = (f32[256]{0:T(256)S(1)}, f32[256]{0:T(256)S(1)}, f32[256]{0:T(256)S(1)}, f32[256]{0:T(256)S(1)}, f32[256]{0:T(256)S(1)}, /*index=...) fusion(f32[256]{0:T(256)S(1)} %bitcast.1449, ...), kind=kLoop, calls=%fused_computation.306 | loop fusion | flops 15872 | bytes 64636 | tf_op jit(solution)/shard_map/eval_jaxpr/sub | solution.py:110
  916.2 17.5 %fusion.127 = f32[1024,1024,1]{1,0,2:T(8,128)} fusion(s32[1024]{0:T(1024)S(1)} %add_select_fusion.2, pred[1024]{0:T(1024)(128)(4,1)S(1)} %iota_compare_fusion.1), kind=kLoop, calls=%fused_computation.160.clone | loop fusion | flops 15728640 | bytes 4199424 | tf_op jit(solution)/shard_map/dot_general | solution.py:126
  933.7 19.8 %select_multiply_fusion = (f32[1024,1024]{1,0:T(8,128)}, f32[1024,1024]{1,0:T(8,128)}) fusion(f32[1024]{0:T(1024)S(1)} %get-tuple-element.794, s32[1024]{0:T(1024)S(1)} %add_select_fusion.2, pred[1024]{0:T(1024)(128)(4,1)S(1)} %iota_compare_fusion.1, f32[1024]{0:T(1024)S(1)} %get-tuple-element.793, f32[1024]{0:T(1024)S(1)} %fusion.79), kind=kLoop, calls=%fused_computation.162 | loop fusion | flops 19922944 | bytes 8406016 | tf_op jit(solution)/shard_map/mul | solution.py:69
  1028.0 54.0 %while.54 = (s32[]{:T(128)}, f32[64,1024]{1,0:T(8,128)S(1)}, f32[64,1024]{1,0:T(8,128)S(1)}, f32[64,1024]{1,0:T(8,128)S(1)}, s32[]{:T(128)}) while((s32[]{:T(128)}, f32[64,1024]{1,0:T(8,128)S(1)}, f32[64,1024]{1,0:T(8,128)S(1)}, f32[64,1024]{1,0:T(8,128)S(1)}, s32[]{:T(128)}) %tuple.606), condition=%wide.region_5.6_spmd, body=%wide.region_4.5_spmd.sunk | while | flops 131074 | bytes 2097253 | solution.py:144
  1119.3 19.3 %all_to_all.72 = f32[4,1,131072]{2,1,0:T(1,128)} all-to-all(f32[4,1,131072]{2,1,0:T(1,128)} %reshape.502), channel_id=1, replica_groups=mesh['ax'=8,'xs'=4] {'xs'}, dimensions={0} | all-to-all | bytes 4194304 | tf_op jit(solution)/shard_map/all_to_all | solution.py:123
  1242.7 70.8 %while.55 = (s32[]{:T(128)}, f32[64,1024]{1,0:T(8,128)S(1)}, f32[64,1024]{1,0:T(8,128)S(1)}, f32[64,1024]{1,0:T(8,128)S(1)}, s32[]{:T(128)}) while((s32[]{:T(128)}, f32[64,1024]{1,0:T(8,128)S(1)}, f32[64,1024]{1,0:T(8,128)S(1)}, f32[64,1024]{1,0:T(8,128)S(1)}, s32[]{:T(128)}) %tuple.612), condition=%wide.region_7.8_spmd, body=%wide.region_6.7_spmd.sunk | while | flops 131074 | bytes 2097253 | solution.py:144
  1242.7 21.0 %collective-permute-start.1 = (f32[64,1024]{1,0:T(8,128)S(1)}, f32[64,1024]{1,0:T(8,128)S(1)}, u32[]{:S(2)}, u32[]{:S(2)}) collective-permute-start(f32[64,1024]{1,0:T(8,128)S(1)} %multiply_add_fusion.7), channel_id=1, source_target_pairs={{0,4},{4,8},{8,12},{12,16},{16,20},{20,24},{24,28},{1,5},{5,9},{9,... | collective-permute-start | bytes 786440 | tf_op jit(solution)/shard_map/while/body/eval_jaxpr/ppermute | solution.py:44
  (388 shorter events, 440.9 us)
Async XLA Ops:
  3.1 842.6 %collective-permute-start.2 = (f32[4,64,1024]{2,1,0:T(8,128)}, f32[4,64,1024]{2,1,0:T(8,128)}, u32[]{:S(2)}, u32[]{:S(2)}) collective-permute-start(f32[4,64,1024]{2,1,0:T(8,128)} %get-tuple-element.587), channel_id=1, source_target_pairs={{0,4},{4,8},{8,12},{12,16},{16,20},{20,24},{24,28},{1,5},{5,9},{9,... | collective-permute-start | bytes 3145736 | tf_op jit(solution)/shard_map/ppermute | solution.py:33
  7.7 840.4 %collective-permute-start.3 = (f32[4,64,1024]{2,1,0:T(8,128)}, f32[4,64,1024]{2,1,0:T(8,128)S(1)}, u32[]{:S(2)}, u32[]{:S(2)}) collective-permute-start(f32[4,64,1024]{2,1,0:T(8,128)} %get-tuple-element.588), channel_id=1, source_target_pairs={{4,0},{8,4},{12,8},{16,12},{20,16},{24,20},{28,24},{5,1},{9,5},{13... | collective-permute-start | bytes 3145736 | tf_op jit(solution)/shard_map/ppermute | solution.py:36
  860.9 28.8 %all-to-all-start = ((f32[4,1,131072]{2,1,0:T(1,128)}), f32[4,1,131072]{2,1,0:T(1,128)S(1)}, u32[]{:S(2)}, u32[]{:S(2)}) async-start(f32[4,1,131072]{2,1,0:T(1,128)} %reshape.500), calls=%async_computation | async-start | bytes 4194304 | tf_op jit(solution)/shard_map/all_to_all | solution.py:123
  886.9 19.9 %copy-start.23 = (f32[256,256]{1,0:T(8,128)}, f32[256,256]{1,0:T(8,128)S(1)}, u32[]{:S(2)}) copy-start(f32[256,256]{1,0:T(8,128)S(1)} %concatenate.77) | copy-start | bytes 786436
  912.4 41.1 %all-to-all-start.1 = ((f32[8,256,256]{2,0,1:T(8,128)}), f32[8,256,256]{2,0,1:T(8,128)S(1)}, u32[]{:S(2)}, u32[]{:S(2)}) async-start(f32[8,256,256]{2,0,1:T(8,128)} %copy.28), calls=%async_computation.1 | async-start | bytes 4194304 | tf_op jit(solution)/shard_map/all_to_all | solution.py:125
  967.9 13.8 %copy-start.10 = (f32[8,64,1024]{2,1,0:T(8,128)S(1)}, f32[8,64,1024]{2,1,0:T(8,128)}, u32[]{:S(2)}) copy-start(f32[8,64,1024]{2,1,0:T(8,128)} %param.12) | copy-start | bytes 6291460
  967.9 13.8 %copy-start.12 = (f32[8,64,1024]{2,1,0:T(8,128)S(1)}, f32[8,64,1024]{2,1,0:T(8,128)}, u32[]{:S(2)}) copy-start(f32[8,64,1024]{2,1,0:T(8,128)} %param.13) | copy-start | bytes 6291460
  1028.1 7.5 collective-permute-start
  1035.6 7.7 collective-permute-start
  1043.4 7.7 collective-permute-start
  1051.1 7.7 collective-permute-start
  1058.8 7.7 collective-permute-start
  1066.6 7.7 collective-permute-start
  1074.3 7.7 collective-permute-start
  1088.4 16.9 %collective-permute-start.5 = (f32[4,64,1024]{2,1,0:T(8,128)S(1)}, f32[4,64,1024]{2,1,0:T(8,128)S(1)}, u32[]{:S(2)}, u32[]{:S(2)}) collective-permute-start(f32[4,64,1024]{2,1,0:T(8,128)S(1)} %get-tuple-element.578), channel_id=1, source_target_pairs={{4,0},{8,4},{12,8},{16,12},{20,16},{24,20},{28,24},{5,1},{9,5},{13... | collective-permute-start | bytes 3145736 | tf_op jit(solution)/shard_map/ppermute | solution.py:36
  1090.3 16.1 %collective-permute-start.4 = (f32[4,64,1024]{2,1,0:T(8,128)S(1)}, f32[4,64,1024]{2,1,0:T(8,128)S(1)}, u32[]{:S(2)}, u32[]{:S(2)}) collective-permute-start(f32[4,64,1024]{2,1,0:T(8,128)S(1)} %get-tuple-element.577), channel_id=1, source_target_pairs={{0,4},{4,8},{8,12},{12,16},{16,20},{20,24},{24,28},{1,5},{5,9},{9,... | collective-permute-start | bytes 3145736 | tf_op jit(solution)/shard_map/ppermute | solution.py:33
  1167.4 22.0 %all-to-all-start.3 = ((f32[8,256,256]{2,0,1:T(8,128)}), f32[8,256,256]{2,0,1:T(8,128)}, u32[]{:S(2)}, u32[]{:S(2)}) async-start(f32[8,256,256]{2,0,1:T(8,128)} %copy.35), calls=%async_computation.3 | async-start | bytes 4194304 | tf_op jit(solution)/shard_map/all_to_all | solution.py:125
  1242.7 24.3 %collective-permute-start.1 = (f32[64,1024]{1,0:T(8,128)S(1)}, f32[64,1024]{1,0:T(8,128)S(1)}, u32[]{:S(2)}, u32[]{:S(2)}) collective-permute-start(f32[64,1024]{1,0:T(8,128)S(1)} %multiply_add_fusion.7), channel_id=1, source_target_pairs={{0,4},{4,8},{8,12},{12,16},{16,20},{20,24},{24,28},{1,5},{5,9},{9,... | collective-permute-start | bytes 786440 | tf_op jit(solution)/shard_map/while/body/eval_jaxpr/ppermute | solution.py:44
  1267.1 7.7 collective-permute-start.1
  1274.9 7.7 collective-permute-start.1
  1282.6 7.7 collective-permute-start.1
  1290.3 7.7 collective-permute-start.1
  1298.1 7.7 collective-permute-start.1
  1305.8 7.7 collective-permute-start.1
  (24 other events, 110.6 us)
where the time goes:
time: 1340 us; the launch traced here: 1320 us
  other arithmetic  440 us (33%)
  loops' own time  421 us (31%)
  local copies, waits for them, and re-layouts  159 us (12%)
  starting transfers between devices  103 us (8%)
  waiting for transfers between devices  60.5 us (5%)
  between operations  59.8 us (4%)
  matrix products  55.5 us (4%)
  blocking collectives  19.3 us (1%)
    another operation x2, loops' own time, body(): lax.linalg.tridiagonal_solve(sub_diag, main_diag, super_diag, jnp.eye(rad...  421 us
    div x8, other arithmetic, body(): lax.linalg.tridiagonal_solve(sub_diag, main_diag, super_diag, jnp.eye(rad...  162 us
    sub x8, other arithmetic, body(): lax.linalg.tridiagonal_solve(sub_diag, main_diag, super_diag, jnp.eye(rad...  158 us
    ppermute x14, starting transfers between devices, from_behind(): lax.ppermute(value, axis, [(source, source + steps) for source in range(i...  77.9 us
    slice x101, local copies, waits for them, and re-layouts, body(): lax.linalg.tridiagonal_solve(sub_diag, main_diag, super_diag, jnp.eye(rad...  48.5 us
    ppermute x14, waiting for transfers between devices, from_behind(): lax.ppermute(value, axis, [(source, source + steps) for source in range(i...  46.1 us
    dot_general x2, other arithmetic, body(): jnp.dot(solved, forward, precision=lax.Precision.HIGHEST, preferred_eleme...  35.1 us
    pad x12, local copies, waits for them, and re-layouts, body(): lax.associative_scan(combine_pairs, (factor, scaled), axis=0)  33.8 us
  transfers between devices with their start and end apart: 21, of which 17 were waited for; matrix products, arithmetic and copies ran while one was open for 33% of the time, Pallas kernels for 0%

commit v1 on v0

v1 whole, which is shorter than its diff:
```python
import functools
import math

import jax
import jax.numpy as jnp
import ml_dtypes
import numpy as np
from jax import lax
from jax.experimental import pallas as pl
from jax.experimental.pallas import tpu as pltpu
from jax.sharding import PartitionSpec as P

CZ = 8
SUBSTEPS = 2
HALO = 4
CHUNK = 16
MESH = pl.DeviceIdType.MESH

axial_weight = 0.2
azimuth_damp = 0.5
diffusion_number = 1.0
stencil_coeffs = (
    -205.0 / 72.0,
    1.6,
    -0.2,
    8.0 / 315.0,
    -1.0 / 560.0,
)


def split_table(table):
    high = table.astype(np.float32).astype(ml_dtypes.bfloat16)
    low = (table - high.astype(np.float64)).astype(np.float32).astype(ml_dtypes.bfloat16)
    return high, low


def radial_tables(cells, groups):
    rows = cells // groups
    index = np.arange(cells, dtype=np.float64)
    radius = index + 0.5
    upper = np.where(index < cells - 1, index + 1.0, 0.0)
    sub = -diffusion_number * index / radius
    sup = -diffusion_number * upper / radius
    full = np.diag(1.0 - sub - sup) + np.diag(sub[1:], -1) + np.diag(sup[:-1], 1)
    local = np.zeros((groups, rows, rows))
    spikes = np.zeros((groups, rows, 2))
    coupling = np.zeros((2 * groups, 2 * groups))
    for d in range(groups):
        first, last = d * rows, (d + 1) * rows - 1
        local[d] = np.linalg.inv(full[first : last + 1, first : last + 1])
        if d > 0:
            spikes[d, :, 0] = -local[d][:, 0] * sub[first]
            coupling[2 * d, 2 * d - 1] = spikes[d, 0, 0]
            coupling[2 * d + 1, 2 * d - 1] = spikes[d, -1, 0]
        if d < groups - 1:
            spikes[d, :, 1] = -local[d][:, -1] * sup[last]
            coupling[2 * d, 2 * d + 2] = spikes[d, 0, 1]
            coupling[2 * d + 1, 2 * d + 2] = spikes[d, -1, 1]
    reduced = np.linalg.inv(np.eye(2 * groups) - coupling)
    mix = np.zeros((groups, 2, 2 * groups))
    for d in range(groups):
        if d > 0:
            mix[d, 0] = reduced[2 * d - 1]
        if d < groups - 1:
            mix[d, 1] = reduced[2 * d + 2]
    return local, spikes, mix


def azimuth_tables(points, cells, groups):
    half, quarter = points // 2, points // 4
    grid = np.arange(half)
    even, odd = 2 * np.arange(quarter), 2 * np.arange(quarter) + 1

    def angle(m):
        return (grid[:, None] * m[None, :] % points) * (2.0 * math.pi / points)

    sine_even = np.sin(angle(even))
    sine_even[:, 0] = np.cos(math.pi * grid)
    table_even = np.concatenate([np.cos(angle(even)), sine_even], axis=1)
    table_odd = np.concatenate([np.cos(angle(odd)), np.sin(angle(odd))], axis=1)
    sine_m = even.copy()
    sine_m[0] = half
    wave = np.concatenate([even, sine_m, odd, odd]).astype(np.float64)
    weight = np.where((wave == 0) | (wave == half), 1.0, 2.0) / points
    radius = np.arange(cells) + 0.5
    damp = weight / (1.0 + azimuth_damp * wave[None, :] ** 2 / radius[:, None] ** 2)
    rate_even = np.where(even > 0, even, 0) * (2.0 * math.pi / points)
    rate_odd = odd * (2.0 * math.pi / points)
    rates = np.broadcast_to(np.concatenate([rate_even, rate_odd]), (8, half))
    return table_even, table_odd, damp.reshape(groups, cells // groups, points), rates


def dot(a, b):
    return jnp.dot(a, b, preferred_element_type=jnp.float32)


def split(x):
    high = x.astype(jnp.bfloat16)
    return high, (x - high.astype(jnp.float32)).astype(jnp.bfloat16)


def dot_table(x, high_table, low_table):
    rows = x.shape[0]
    high, low = split(x)
    both = dot(jnp.concatenate([high, low], axis=0), high_table)
    return both[:rows] + (both[rows:] + dot(high, low_table))


def kernel(
    n_ax, n_xs,
    u_hbm, rate_hbm, swirl_hbm, dft_hbm, local_hbm, spikes_hbm, damp_hbm, rates_hbm, mix,
    out_ref,
    field, rate_ref, swirl_ref, dft, local, spikes, damp, rates,
    halo, inc, bound, solved, part, decay, lines, qe, qo, corr,
    load_sem, halo_send, halo_recv, inc_send, inc_recv, bound_send, bound_recv,
):
    planes, rows_all, points = field.shape
    half, quarter = points // 2, points // 4
    chunk = min(CHUNK, rows_all)
    chunks = rows_all // chunk
    ax, xs = lax.axis_index("ax"), lax.axis_index("xs")
    ahead, behind = lax.rem(ax + 1, n_ax), lax.rem(ax + n_ax - 1, n_ax)
    has_behind, has_ahead = ax > 0, ax < n_ax - 1

    loads = [
        pltpu.make_async_copy(source, target, load_sem.at[i])
        for i, (source, target) in enumerate(
            [
                (u_hbm, field),
                (local_hbm.at[xs], local),
                (spikes_hbm.at[xs], spikes),
                (dft_hbm, dft),
                (damp_hbm.at[xs], damp),
                (rates_hbm, rates),
                (swirl_hbm, swirl_ref),
                (rate_hbm, rate_ref),
            ]
        )
    ]
    for load in loads:
        load.start()

    barrier = pltpu.get_barrier_semaphore()

    @pl.when(has_behind)
    def _():
        pl.semaphore_signal(barrier, inc=1, device_id=(behind, xs), device_id_type=MESH)

    @pl.when(has_ahead)
    def _():
        pl.semaphore_signal(barrier, inc=1, device_id=(ahead, xs), device_id_type=MESH)

    for i in range(1, n_xs):
        pl.semaphore_signal(
            barrier, inc=1, device_id=(ax, lax.rem(xs + i, n_xs)), device_id_type=MESH
        )
    peers = n_xs - 1 + has_behind.astype(jnp.int32) + has_ahead.astype(jnp.int32)

    def rows_of(c):
        return pl.ds(pl.multiple_of(c * chunk, chunk), chunk)

    def halo_copy(s, side, c):
        start = planes - HALO if side == 0 else 0
        return pltpu.make_async_remote_copy(
            src_ref=solved.at[s, pl.ds(start, HALO), rows_of(c), :],
            dst_ref=halo.at[s, side, :, rows_of(c), :],
            send_sem=halo_send.at[s, side, c],
            recv_sem=halo_recv.at[s, side, c],
            device_id=(ahead if side == 0 else behind, xs),
            device_id_type=MESH,
        )

    def start_halo(s, c):
        @pl.when(has_ahead)
        def _():
            halo_copy(s, 0, c).start()

        @pl.when(has_behind)
        def _():
            halo_copy(s, 1, c).start()

    def relay_copy(s, c):
        source = field if s == 0 else out_ref
        return pltpu.make_async_remote_copy(
            src_ref=source.at[planes - 1, rows_of(c), :],
            dst_ref=inc.at[s, rows_of(c), :],
            send_sem=inc_send.at[s, c],
            recv_sem=inc_recv.at[s, c],
            device_id=(ahead, xs),
            device_id_type=MESH,
        )

    def bound_copy(s, i, owner):
        return pltpu.make_async_remote_copy(
            src_ref=bound.at[s, owner],
            dst_ref=bound.at[s, owner],
            send_sem=bound_send.at[s, i - 1],
            recv_sem=bound_recv.at[s, i - 1],
            device_id=(ax, lax.rem(xs + i, n_xs)),
            device_id_type=MESH,
        )

    def loop(body):
        lax.fori_loop(0, chunks, lambda c, carry: (body(c), carry)[1], 0)

    @pl.when(jnp.logical_not(has_behind))
    def _():
        halo[:, 0] = jnp.zeros_like(halo[:, 0])
        inc[...] = jnp.zeros_like(inc)

    @pl.when(jnp.logical_not(has_ahead))
    def _():
        halo[:, 1] = jnp.zeros_like(halo[:, 1])

    group = local.shape[1] // rows_all
    depth = group * rows_all
    for load in loads[:3]:
        load.wait()

    for s in range(SUBSTEPS):
        result = field if s == 0 else out_ref

        for first in range(0, planes, group):
            for column in range(0, points, 256):
                columns = slice(column, column + 256)
                x = field[first : first + group, :, columns].reshape(depth, 256)
                high, low = split(x)
                both = dot(local[...], high)
                x = both[:depth] + (both[depth:] + dot(local[:depth, :], low))
                for k in range(group):
                    here = x[k * rows_all : (k + 1) * rows_all]
                    solved[s, first + k, :, columns] = here
                    bound[s, xs, first + k : first + k + 1, columns] = here[:1]
                    place = planes + first + k
                    bound[s, xs, place : place + 1, columns] = here[rows_all - 1 :]
        if s == 0:
            pl.semaphore_wait(barrier, peers)
        for i in range(1, n_xs):
            bound_copy(s, i, xs).start()
        for i in range(1, n_xs):
            bound_copy(s, i, lax.rem(xs + n_xs - i, n_xs)).wait_recv()
        for side in range(2):
            total = jnp.zeros((planes, points), jnp.float32)
            for j in range(2 * n_xs):
                place = (j % 2) * planes
                total += mix[(xs * 2 + side) * 2 * n_xs + j] * bound[s, j // 2, place : place + planes, :]
            corr[side] = total

        def correct(c):
            rows = rows_of(c)
            spike = spikes[rows, :]
            left, right = spike[:, 0:1], spike[:, 1:2]
            for k in range(planes):
                solved[s, k, rows, :] += left * corr[0, k : k + 1, :] + right * corr[1, k : k + 1, :]
            start_halo(s, c)

        loop(correct)
        if s == 0:
            for load in loads[3:]:
                load.wait()

        def finish_rows(c):
            rows = rows_of(c)

            @pl.when(has_behind)
            def _():
                halo_copy(s, 0, c).wait_recv()

            @pl.when(has_ahead)
            def _():
                halo_copy(s, 1, c).wait_recv()

            def plane(k):
                if k < 0:
                    return halo[s, 0, k + HALO, rows, :]
                if k >= planes:
                    return halo[s, 1, k - planes, rows, :]
                return solved[s, k, rows, :]

            for k in range(planes):
                total = (1.0 + axial_weight * stencil_coeffs[0]) * plane(k)
                for d in range(1, HALO + 1):
                    total += axial_weight * stencil_coeffs[d] * (plane(k - d) + plane(k + d))
                lines[k * chunk : (k + 1) * chunk, :] = total
            low, high = lines[:, :half], lines[:, half:]
            even = dot_table(low + high, dft[0], dft[1])
            odd = dot_table(low - high, dft[2], dft[3])
            scale = damp[rows, :]
            rate_even, rate_odd = rates[0:1, :quarter], rates[0:1, quarter:]
            for k in range(planes):
                here = slice(k * chunk, (k + 1) * chunk)
                there = slice((planes + k) * chunk, (planes + k + 1) * chunk)
                value_even = even[here] * scale[:, :half]
                value_odd = odd[here] * scale[:, half:]
                qe[here, :] = value_even
                qo[here, :] = value_odd
                qe[there, :quarter] = rate_even * value_even[:, quarter:]
                qe[there, quarter:] = -rate_even * value_even[:, :quarter]
                qo[there, :quarter] = rate_odd * value_odd[:, quarter:]
                qo[there, quarter:] = -rate_odd * value_odd[:, :quarter]
            qe[...] = dot_table(qe[...], dft[4], dft[5])
            qo[...] = dot_table(qo[...], dft[6], dft[7])
            for side in range(2):
                columns = slice(side * half, (side + 1) * half)
                value = jnp.zeros((chunk, half), jnp.float32)
                product = jnp.ones((chunk, half), jnp.float32)
                for k in range(planes):
                    here = slice(k * chunk, (k + 1) * chunk)
                    there = slice((planes + k) * chunk, (planes + k + 1) * chunk)
                    if side == 0:
                        smooth, slope = qe[here, :] + qo[here, :], qe[there, :] + qo[there, :]
                    else:
                        smooth, slope = qe[here, :] - qo[here, :], qe[there, :] - qo[there, :]
                    courant = CZ * rate_ref[k, rows, columns]
                    inverse = 1.0 / (1.0 + courant)
                    factor = courant * inverse
                    value = inverse * (smooth - swirl_ref[k, rows, columns] * slope) + factor * value
                    product = factor * product
                    part[k, :, columns] = value
                    decay[k, :, columns] = product

            @pl.when(has_behind)
            def _():
                relay_copy(s, c).wait_recv()

            last = planes - 1
            entering = inc[s, rows, :]
            result[last, rows, :] = part[last] + decay[last] * entering

            @pl.when(has_ahead)
            def _():
                relay_copy(s, c).start()

            for k in range(last):
                result[k, rows, :] = part[k] + decay[k] * entering

        loop(finish_rows)

    for s in range(SUBSTEPS):

        def finish(c):
            @pl.when(has_ahead)
            def _():
                halo_copy(s, 0, c).wait_send()
                relay_copy(s, c).wait_send()

            @pl.when(has_behind)
            def _():
                halo_copy(s, 1, c).wait_send()

        loop(finish)
        for i in range(1, n_xs):
            bound_copy(s, i, xs).wait_send()


def solution(mesh):
    n_ax, n_xs = mesh.shape["ax"], mesh.shape["xs"]

    def body(scalar, axial_rate, swirl_rate):
        planes, rows, points = scalar.shape
        cells = rows * n_xs
        chunk = min(CHUNK, rows)
        chunks = rows // chunk
        half = points // 2
        local, spikes, mix = radial_tables(cells, n_xs)
        even, odd, damp, rates = azimuth_tables(points, cells, n_xs)
        pairs = [split_table(x) for x in (even, odd, even.T, odd.T)]
        dft = np.stack([x for pair in pairs for x in pair])
        group = min(planes, 256 // rows)
        blocks = np.stack([np.kron(np.eye(group), x) for x in local])
        blocks = np.concatenate(split_table(blocks), axis=1)
        spikes = np.pad(spikes, ((0, 0), (0, 0), (0, 126))).astype(np.float32)
        tables = [dft, blocks, spikes, damp.astype(np.float32), rates.astype(np.float32)]
        f32 = jnp.float32
        block = pltpu.VMEM((planes, rows, points), f32)
        part = pltpu.VMEM((planes, chunk, points), f32)
        pair = pltpu.VMEM((2 * planes * chunk, half), f32)
        dma = pltpu.SemaphoreType.DMA
        return pl.pallas_call(
            functools.partial(kernel, n_ax, n_xs),
            out_shape=jax.ShapeDtypeStruct(scalar.shape, f32),
            in_specs=[pl.BlockSpec(memory_space=pl.ANY)] * (3 + len(tables))
            + [pl.BlockSpec(memory_space=pltpu.SMEM)],
            out_specs=pl.BlockSpec(memory_space=pltpu.VMEM),
            scratch_shapes=[
                block, block, block,
                pltpu.VMEM(dft.shape, jnp.bfloat16),
                pltpu.VMEM(blocks.shape[1:], jnp.bfloat16),
                pltpu.VMEM(spikes.shape[1:], f32),
                pltpu.VMEM(damp.shape[1:], f32),
                pltpu.VMEM(rates.shape, f32),
                pltpu.VMEM((SUBSTEPS, 2, HALO, rows, points), f32),
                pltpu.VMEM((SUBSTEPS, rows, points), f32),
                pltpu.VMEM((SUBSTEPS, n_xs, 2 * planes, points), f32),
                pltpu.VMEM((SUBSTEPS, planes, rows, points), f32),
                part, part,
                pltpu.VMEM((planes * chunk, points), f32),
                pair, pair,
                pltpu.VMEM((2, planes, points), f32),
                dma((8,)),
                dma((SUBSTEPS, 2, chunks)), dma((SUBSTEPS, 2, chunks)),
                dma((SUBSTEPS, chunks)), dma((SUBSTEPS, chunks)),
                dma((SUBSTEPS, n_xs - 1)), dma((SUBSTEPS, n_xs - 1)),
            ],
            compiler_params=pltpu.CompilerParams(
                collective_id=0, has_side_effects=True, vmem_limit_bytes=62 * 2**20
            ),
        )(
            scalar, axial_rate, swirl_rate,
            *[jnp.asarray(t) for t in tables],
            jnp.asarray(mix.reshape(-1).astype(np.float32)),
        )

    return jax.shard_map(
        body,
        mesh=mesh,
        in_specs=(P("ax", "xs", None), P("ax", "xs", None), P("ax", "xs", None)),
        out_specs=P("ax", "xs", None),
        check_vma=False,
    )
```

time: 1340 us -> 65 us (0.05)
  the two profiles are of different devices: /device:TPU:1 before, /device:TPU:25 now
where the time goes in v1:
time: 65 us; the launch traced here: 64.9 us
  Pallas kernels  61.7 us (95%)
  local copies, waits for them, and re-layouts  3.16 us (5%)
    pallas_call x1, Pallas kernels, body(): pl.pallas_call(functools.partial(kernel, n_ax, n_xs), out_shape=jax.Shape...  61.7 us
    unnamed x1, local copies, waits for them, and re-layouts  3.16 us

profile of v1, /device:TPU:25, one launch (start us, length us, event | category | flops | bytes accessed | tf_op | source)
XLA Modules:
  0.0 64.9 jit_solution(1787913149149710652)
XLA Ops:
  0.0 61.7 %shard_map.91 = f32[8,64,1024]{2,1,0:T(8,128)} custom-call(f32[8,64,1024]{2,1,0:T(8,128)} %u_hbm.1, f32[8,64,1024]{2,1,0:T(8,128)} %rate_hbm.1, f32[8,64,1024]{2,1,0:T(8,128)} %swirl_hbm.1, bf16[8,512,512]{2,1,0:T(8,128)(2,1)} %constant.12.clone.dft_hbm, bf16[4,512,256]{2,1,0:T(8,128)(2,1)} %constant.13.clone.local_hbm, ...), custom_call_target="tpu_custom_call" | custom-call | tf_op jit(solution)/shard_map/pallas_call | solution.py:379
  61.7 3.2 %copy.11 = f32[8,64,1024]{2,1,0:T(8,128)} copy(f32[8,64,1024]{2,1,0:T(8,128)} %shard_map.91) | data formatting | bytes 4194304

commit v2 on v1

--- a/solution.py
+++ b/solution.py
@@ -316,8 +316,13 @@
                     factor = courant * inverse
                     value = inverse * (smooth - swirl_ref[k, rows, columns] * slope) + factor * value
                     product = factor * product
-                    part[k, :, columns] = value
-                    decay[k, :, columns] = product
+                    part[k, rows, columns] = value
+                    decay[k, rows, columns] = product
+
+        loop(finish_rows)
+
+        def relay(c):
+            rows = rows_of(c)
 
             @pl.when(has_behind)
             def _():
@@ -325,16 +330,16 @@
 
             last = planes - 1
             entering = inc[s, rows, :]
-            result[last, rows, :] = part[last] + decay[last] * entering
+            result[last, rows, :] = part[last, rows, :] + decay[last, rows, :] * entering
 
             @pl.when(has_ahead)
             def _():
                 relay_copy(s, c).start()
 
             for k in range(last):
-                result[k, rows, :] = part[k] + decay[k] * entering
-
-        loop(finish_rows)
+                result[k, rows, :] = part[k, rows, :] + decay[k, rows, :] * entering
+
+        loop(relay)
 
     for s in range(SUBSTEPS):
 
@@ -373,7 +378,6 @@
         tables = [dft, blocks, spikes, damp.astype(np.float32), rates.astype(np.float32)]
         f32 = jnp.float32
         block = pltpu.VMEM((planes, rows, points), f32)
-        part = pltpu.VMEM((planes, chunk, points), f32)
         pair = pltpu.VMEM((2 * planes * chunk, half), f32)
         dma = pltpu.SemaphoreType.DMA
         return pl.pallas_call(
@@ -393,7 +397,7 @@
                 pltpu.VMEM((SUBSTEPS, rows, points), f32),
                 pltpu.VMEM((SUBSTEPS, n_xs, 2 * planes, points), f32),
                 pltpu.VMEM((SUBSTEPS, planes, rows, points), f32),
-                part, part,
+                block, block,
                 pltpu.VMEM((planes * chunk, points), f32),
                 pair, pair,
                 pltpu.VMEM((2, planes, points), f32),

time: 65 us -> 69.3 us (1.066)
  Pallas kernels: 61.7 us -> 66 us
    pallas_call x1, Pallas kernels: 61.7 us -> 66 us  [body(): pl.pallas_call(functools.partial(kernel, n_ax, n_xs), out_shape=jax.Shape...]
where the time goes in v2:
time: 69.3 us; the launch traced here: 69.1 us
  Pallas kernels  66 us (95%)
  local copies, waits for them, and re-layouts  3.16 us (5%)
    pallas_call x1, Pallas kernels, body(): pl.pallas_call(functools.partial(kernel, n_ax, n_xs), out_shape=jax.Shape...  66 us
    unnamed x1, local copies, waits for them, and re-layouts  3.16 us

profile of v2, /device:TPU:25, one launch (start us, length us, event | category | flops | bytes accessed | tf_op | source)
XLA Modules:
  0.0 69.1 jit_solution(15032800284405428221)
XLA Ops:
  0.0 66.0 %shard_map.91 = f32[8,64,1024]{2,1,0:T(8,128)} custom-call(f32[8,64,1024]{2,1,0:T(8,128)} %u_hbm.1, f32[8,64,1024]{2,1,0:T(8,128)} %rate_hbm.1, f32[8,64,1024]{2,1,0:T(8,128)} %swirl_hbm.1, bf16[8,512,512]{2,1,0:T(8,128)(2,1)} %constant.12.clone.dft_hbm, bf16[4,512,256]{2,1,0:T(8,128)(2,1)} %constant.13.clone.local_hbm, ...), custom_call_target="tpu_custom_call" | custom-call | tf_op jit(solution)/shard_map/pallas_call | solution.py:383
  66.0 3.2 %copy.11 = f32[8,64,1024]{2,1,0:T(8,128)} copy(f32[8,64,1024]{2,1,0:T(8,128)} %shard_map.91) | data formatting | bytes 4194304

commit v3 on v1

--- a/solution.py
+++ b/solution.py
@@ -66,6 +66,40 @@
     return local, spikes, mix
 
 
+def chunk_tables(cells, groups, chunk):
+    rows = cells // groups
+    chunks = rows // chunk
+    edges = 2 * chunks
+    local, spikes, _ = radial_tables(cells, groups * chunks)
+    _, outer, mix = radial_tables(cells, groups)
+    weights = []
+    for d in range(groups):
+        coupling = np.zeros((edges, edges))
+        for c in range(chunks):
+            spike = spikes[d * chunks + c]
+            for side, row in ((0, 0), (1, -1)):
+                if c > 0:
+                    coupling[2 * c + side, 2 * c - 1] = spike[row, 0]
+                if c < chunks - 1:
+                    coupling[2 * c + side, 2 * c + 2] = spike[row, 1]
+        inner = np.linalg.inv(np.eye(edges) - coupling)
+        near = np.zeros((edges, edges + 2))
+        for c in range(chunks):
+            if c > 0:
+                near[2 * c, :edges] = inner[2 * c - 1]
+                near[2 * c, edges:] = outer[d, c * chunk - 1]
+            else:
+                near[0, edges] = 1.0
+            if c < chunks - 1:
+                near[2 * c + 1, :edges] = inner[2 * c + 2]
+                near[2 * c + 1, edges:] = outer[d, (c + 1) * chunk]
+            else:
+                near[2 * c + 1, edges + 1] = 1.0
+        ends = inner[[0, -1]]
+        weights.append(np.concatenate([ends.reshape(-1), mix[d].reshape(-1), near.reshape(-1)]))
+    return local, spikes.reshape(groups, rows, 2), np.stack(weights)
+
+
 def azimuth_tables(points, cells, groups):
     half, quarter = points // 2, points // 4
     grid = np.arange(half)
@@ -111,8 +145,8 @@
     u_hbm, rate_hbm, swirl_hbm, dft_hbm, local_hbm, spikes_hbm, damp_hbm, rates_hbm, mix,
     out_ref,
     field, rate_ref, swirl_ref, dft, local, spikes, damp, rates,
-    halo, inc, bound, solved, part, decay, lines, qe, qo, corr,
-    load_sem, halo_send, halo_recv, inc_send, inc_recv, bound_send, bound_recv,
+    halo, inc, bound, solved, part, decay, lines, qe, qo, corr, edge, pack, side_halo, extended,
+    load_sem, halo_send, halo_recv, side_send, side_recv, inc_send, inc_recv, bound_send, bound_recv,
 ):
     planes, rows_all, points = field.shape
     half, quarter = points // 2, points // 4
@@ -179,6 +213,16 @@
         def _():
             halo_copy(s, 1, c).start()
 
+    def side_copy(s, side):
+        return pltpu.make_async_remote_copy(
+            src_ref=pack.at[s, side],
+            dst_ref=side_halo.at[s, side],
+            send_sem=side_send.at[s, side],
+            recv_sem=side_recv.at[s, side],
+            device_id=(ahead if side == 0 else behind, xs),
+            device_id_type=MESH,
+        )
+
     def relay_copy(s, c):
         source = field if s == 0 else out_ref
         return pltpu.make_async_remote_copy(
@@ -206,58 +250,92 @@
     @pl.when(jnp.logical_not(has_behind))
     def _():
         halo[:, 0] = jnp.zeros_like(halo[:, 0])
+        side_halo[:, 0] = jnp.zeros_like(side_halo[:, 0])
         inc[...] = jnp.zeros_like(inc)
 
     @pl.when(jnp.logical_not(has_ahead))
     def _():
         halo[:, 1] = jnp.zeros_like(halo[:, 1])
-
-    group = local.shape[1] // rows_all
-    depth = group * rows_all
-    for load in loads[:3]:
-        load.wait()
-
-    for s in range(SUBSTEPS):
-        result = field if s == 0 else out_ref
-
-        for first in range(0, planes, group):
-            for column in range(0, points, 256):
-                columns = slice(column, column + 256)
-                x = field[first : first + group, :, columns].reshape(depth, 256)
-                high, low = split(x)
-                both = dot(local[...], high)
-                x = both[:depth] + (both[depth:] + dot(local[:depth, :], low))
-                for k in range(group):
-                    here = x[k * rows_all : (k + 1) * rows_all]
-                    solved[s, first + k, :, columns] = here
-                    bound[s, xs, first + k : first + k + 1, columns] = here[:1]
-                    place = planes + first + k
-                    bound[s, xs, place : place + 1, columns] = here[rows_all - 1 :]
+        side_halo[:, 1] = jnp.zeros_like(side_halo[:, 1])
+
+    edges = 2 * chunks
+    near_at = 2 * edges + 4 * n_xs
+    stride = near_at + edges * (edges + 2)
+
+    def solve_chunk(s, c):
+        rows = rows_of(c)
+        depth = planes * chunk
+        for column in range(0, points, half):
+            columns = slice(column, column + half)
+            high, low = split(field[:, rows, columns].reshape(depth, half))
+            both = dot(local[c], high)
+            x = both[:depth] + (both[depth:] + dot(local[c, :depth, :], low))
+            for k in range(planes):
+                here = x[k * chunk : (k + 1) * chunk]
+                solved[s, k, rows, columns] = here
+                edge[c, 0, k : k + 1, columns] = here[:1]
+                edge[c, 1, k : k + 1, columns] = here[chunk - 1 :]
+
+    def mixed(start, terms):
+        total = jnp.zeros((planes, points), jnp.float32)
+        for j, term in enumerate(terms):
+            total += mix[xs * stride + start + j] * term()
+        return total
+
+    def join_chunks(s):
+        inner = [lambda j=j: edge[j // 2, j % 2] for j in range(edges)]
+        outer = [lambda j=j: bound[s, j // 2, (j % 2) * planes : (j % 2 + 1) * planes] for j in range(2 * n_xs)]
+        for side in range(2):
+            bound[s, xs, side * planes : (side + 1) * planes, :] = mixed(side * edges, inner)
         if s == 0:
             pl.semaphore_wait(barrier, peers)
+            lax.fori_loop(0, early[0], lambda c, carry: (start_halo(0, c), carry)[1], 0)
         for i in range(1, n_xs):
             bound_copy(s, i, xs).start()
         for i in range(1, n_xs):
             bound_copy(s, i, lax.rem(xs + n_xs - i, n_xs)).wait_recv()
         for side in range(2):
-            total = jnp.zeros((planes, points), jnp.float32)
-            for j in range(2 * n_xs):
-                place = (j % 2) * planes
-                total += mix[(xs * 2 + side) * 2 * n_xs + j] * bound[s, j // 2, place : place + planes, :]
-            corr[side] = total
-
-        def correct(c):
-            rows = rows_of(c)
-            spike = spikes[rows, :]
-            left, right = spike[:, 0:1], spike[:, 1:2]
-            for k in range(planes):
-                solved[s, k, rows, :] += left * corr[0, k : k + 1, :] + right * corr[1, k : k + 1, :]
-            start_halo(s, c)
-
-        loop(correct)
+            corr[edges + side] = mixed(2 * edges + side * 2 * n_xs, outer)
+        inner += [lambda: corr[edges], lambda: corr[edges + 1]]
+        for c in range(chunks):
+            values = []
+            for side in range(2):
+                j = 2 * c + side
+                value = mixed(near_at + j * (edges + 2), inner)
+                corr[j] = value
+                values.append(value)
+            pack[s, 0, c] = jnp.concatenate([x[planes - HALO :] for x in values], axis=0)
+            pack[s, 1, c] = jnp.concatenate([x[:HALO] for x in values], axis=0)
+
+        @pl.when(has_ahead)
+        def _():
+            side_copy(s, 0).start()
+
+        @pl.when(has_behind)
+        def _():
+            side_copy(s, 1).start()
+
+        lax.fori_loop(early[s], chunks, lambda c, carry: (start_halo(s, c), carry)[1], 0)
+
+    early = (min(1, chunks - 1), chunks - 1)
+    for load in loads[:3]:
+        load.wait()
+    loop(lambda c: solve_chunk(0, c))
+
+    for s in range(SUBSTEPS):
+        result = field if s == 0 else out_ref
+        join_chunks(s)
         if s == 0:
             for load in loads[3:]:
                 load.wait()
+
+        @pl.when(has_behind)
+        def _():
+            side_copy(s, 0).wait_recv()
+
+        @pl.when(has_ahead)
+        def _():
+            side_copy(s, 1).wait_recv()
 
         def finish_rows(c):
             rows = rows_of(c)
@@ -277,10 +355,26 @@
                     return halo[s, 1, k - planes, rows, :]
                 return solved[s, k, rows, :]
 
+            centre = 1.0 + axial_weight * stencil_coeffs[0]
+            spike = spikes[rows, :]
+            for side in range(2):
+                extended[side, :HALO] = side_halo[s, 0, c, side * HALO : (side + 1) * HALO]
+                extended[side, HALO : HALO + planes] = corr[2 * c + side]
+                extended[side, HALO + planes :] = side_halo[s, 1, c, side * HALO : (side + 1) * HALO]
+            sides = []
+            for side in range(2):
+                total = centre * extended[side, HALO : HALO + planes]
+                for d in range(1, HALO + 1):
+                    total += axial_weight * stencil_coeffs[d] * (
+                        extended[side, HALO - d : HALO - d + planes]
+                        + extended[side, HALO + d : HALO + d + planes]
+                    )
+                sides.append(total)
             for k in range(planes):
-                total = (1.0 + axial_weight * stencil_coeffs[0]) * plane(k)
+                total = centre * plane(k)
                 for d in range(1, HALO + 1):
                     total += axial_weight * stencil_coeffs[d] * (plane(k - d) + plane(k + d))
+                total += spike[:, 0:1] * sides[0][k : k + 1] + spike[:, 1:2] * sides[1][k : k + 1]
                 lines[k * chunk : (k + 1) * chunk, :] = total
             low, high = lines[:, :half], lines[:, half:]
             even = dot_table(low + high, dft[0], dft[1])
@@ -333,6 +427,12 @@
 
             for k in range(last):
                 result[k, rows, :] = part[k] + decay[k] * entering
+            if s + 1 < SUBSTEPS:
+                solve_chunk(s + 1, c)
+
+                @pl.when(c < early[s + 1])
+                def _():
+                    start_halo(s + 1, c)
 
         loop(finish_rows)
 
@@ -349,6 +449,15 @@
                 halo_copy(s, 1, c).wait_send()
 
         loop(finish)
+
+        @pl.when(has_ahead)
+        def _():
+            side_copy(s, 0).wait_send()
+
+        @pl.when(has_behind)
+        def _():
+            side_copy(s, 1).wait_send()
+
         for i in range(1, n_xs):
             bound_copy(s, i, xs).wait_send()
 
@@ -362,13 +471,13 @@
         chunk = min(CHUNK, rows)
         chunks = rows // chunk
         half = points // 2
-        local, spikes, mix = radial_tables(cells, n_xs)
+        local, spikes, mix = chunk_tables(cells, n_xs, chunk)
         even, odd, damp, rates = azimuth_tables(points, cells, n_xs)
         pairs = [split_table(x) for x in (even, odd, even.T, odd.T)]
         dft = np.stack([x for pair in pairs for x in pair])
-        group = min(planes, 256 // rows)
-        blocks = np.stack([np.kron(np.eye(group), x) for x in local])
+        blocks = np.stack([np.kron(np.eye(planes), x) for x in local])
         blocks = np.concatenate(split_table(blocks), axis=1)
+        blocks = blocks.reshape((n_xs, chunks) + blocks.shape[1:])
         spikes = np.pad(spikes, ((0, 0), (0, 0), (0, 126))).astype(np.float32)
         tables = [dft, blocks, spikes, damp.astype(np.float32), rates.astype(np.float32)]
         f32 = jnp.float32
@@ -396,9 +505,14 @@
                 part, part,
                 pltpu.VMEM((planes * chunk, points), f32),
                 pair, pair,
-                pltpu.VMEM((2, planes, points), f32),
+                pltpu.VMEM((2 * chunks + 2, planes, points), f32),
+                pltpu.VMEM((chunks, 2, planes, points), f32),
+                pltpu.VMEM((SUBSTEPS, 2, chunks, 2 * HALO, points), f32),
+                pltpu.VMEM((SUBSTEPS, 2, chunks, 2 * HALO, points), f32),
+                pltpu.VMEM((2, planes + 2 * HALO, points), f32),
                 dma((8,)),
                 dma((SUBSTEPS, 2, chunks)), dma((SUBSTEPS, 2, chunks)),
+                dma((SUBSTEPS, 2)), dma((SUBSTEPS, 2)),
                 dma((SUBSTEPS, chunks)), dma((SUBSTEPS, chunks)),
                 dma((SUBSTEPS, n_xs - 1)), dma((SUBSTEPS, n_xs - 1)),
             ],

time: 65 us -> 65.5 us (level)
  no operation moved by 1% of the time
where the time goes in v3:
time: 65.5 us; the launch traced here: 65.4 us
  Pallas kernels  62.2 us (95%)
  local copies, waits for them, and re-layouts  3.16 us (5%)
    pallas_call x1, Pallas kernels, body(): pl.pallas_call(functools.partial(kernel, n_ax, n_xs), out_shape=jax.Shape...  62.2 us
    unnamed x1, local copies, waits for them, and re-layouts  3.16 us

profile of v3, /device:TPU:25, one launch (start us, length us, event | category | flops | bytes accessed | tf_op | source)
XLA Modules:
  0.0 65.4 jit_solution(4571918503224577201)
XLA Ops:
  0.0 62.2 %shard_map.91 = f32[8,64,1024]{2,1,0:T(8,128)} custom-call(f32[8,64,1024]{2,1,0:T(8,128)} %u_hbm.1, f32[8,64,1024]{2,1,0:T(8,128)} %rate_hbm.1, f32[8,64,1024]{2,1,0:T(8,128)} %swirl_hbm.1, bf16[8,512,512]{2,1,0:T(8,128)(2,1)} %constant.12.clone.dft_hbm, bf16[4,4,256,128]{3,2,1,0:T(8,128)(2,1)} %constant.13.clone.local_hbm, ...), custom_call_target="tpu_custom_call" | custom-call | tf_op jit(solution)/shard_map/pallas_call | solution.py:488
  62.2 3.2 %copy.11 = f32[8,64,1024]{2,1,0:T(8,128)} copy(f32[8,64,1024]{2,1,0:T(8,128)} %shard_map.91) | data formatting | bytes 4194304

commit v4 on v3

--- a/solution.py
+++ b/solution.py
@@ -315,7 +315,8 @@
         def _():
             side_copy(s, 1).start()
 
-        lax.fori_loop(early[s], chunks, lambda c, carry: (start_halo(s, c), carry)[1], 0)
+        late = min(2, chunks) if s == 0 else chunks
+        lax.fori_loop(early[s], late, lambda c, carry: (start_halo(s, c), carry)[1], 0)
 
     early = (min(1, chunks - 1), chunks - 1)
     for load in loads[:3]:
@@ -347,6 +348,12 @@
             @pl.when(has_ahead)
             def _():
                 halo_copy(s, 1, c).wait_recv()
+
+            if s == 0:
+
+                @pl.when(c + 2 < chunks)
+                def _():
+                    start_halo(s, c + 2)
 
             def plane(k):
                 if k < 0:

time: 65.5 us -> 66.6 us (1.017)
  Pallas kernels: 62.2 us -> 63.3 us
    pallas_call x1, Pallas kernels: 62.2 us -> 63.3 us  [body(): pl.pallas_call(functools.partial(kernel, n_ax, n_xs), out_shape=jax.Shape...]
where the time goes in v4:
time: 66.6 us; the launch traced here: 66.4 us
  Pallas kernels  63.3 us (95%)
  local copies, waits for them, and re-layouts  3.16 us (5%)
    pallas_call x1, Pallas kernels, body(): pl.pallas_call(functools.partial(kernel, n_ax, n_xs), out_shape=jax.Shape...  63.3 us
    unnamed x1, local copies, waits for them, and re-layouts  3.16 us

profile of v4, /device:TPU:25, one launch (start us, length us, event | category | flops | bytes accessed | tf_op | source)
XLA Modules:
  0.0 66.4 jit_solution(1954898089765373709)
XLA Ops:
  0.0 63.3 %shard_map.91 = f32[8,64,1024]{2,1,0:T(8,128)} custom-call(f32[8,64,1024]{2,1,0:T(8,128)} %u_hbm.1, f32[8,64,1024]{2,1,0:T(8,128)} %rate_hbm.1, f32[8,64,1024]{2,1,0:T(8,128)} %swirl_hbm.1, bf16[8,512,512]{2,1,0:T(8,128)(2,1)} %constant.12.clone.dft_hbm, bf16[4,4,256,128]{3,2,1,0:T(8,128)(2,1)} %constant.13.clone.local_hbm, ...), custom_call_target="tpu_custom_call" | custom-call | tf_op jit(solution)/shard_map/pallas_call | solution.py:495
  63.3 3.2 %copy.11 = f32[8,64,1024]{2,1,0:T(8,128)} copy(f32[8,64,1024]{2,1,0:T(8,128)} %shard_map.91) | data formatting | bytes 4194304
